TPU v7x, 128 devices: a whole 4x4x4 slice. The times are simulated.
128 devices in a mesh: row: 8 (over z, core), col: 16 (over x, y).
Axes of the slice: x: 4, y: 4, z: 4, core: 2. Of those that a mesh axis runs over, the one named last changes fastest.
Arguments:
- kernel: float32 [8192, 8192], P('row', 'col'), as said below
Outputs:
- factored: float32 [8192, 8192], P('row', 'col')
Inputs may be any that keep to these rules, and one draw needn't show every extreme that they name: kernel stores a symmetric positive definite matrix in the tile order of the steps.
All inputs are finite; a program needn't handle non-finite values.
Results may differ from a plain program's by a relative error of at most 0.0003.
Values sent between devices are 32-bit elements; how exact they have to be, the bound alone decides.
A program may use at most 128 MiB of HBM per device.

v0:
```python
import jax
import jax.numpy as jnp
from jax import lax
from jax.sharding import PartitionSpec as P

TILE = 512


def broadcast(x, axis, root):
    mine = lax.axis_index(axis) == root
    return lax.psum(jnp.where(mine, x, jnp.zeros_like(x)), axis)


def solve_rows(factor, values):
    return jax.scipy.linalg.solve_triangular(factor, values.T, lower=True).T


def factor_blocks(square):
    size_total = square.shape[0]
    step_cols = min(128, size_total)
    contract = (((1,), (1,)), ((), ()))
    result = jnp.zeros_like(square)
    for start in range(0, size_total, step_cols):
        finish = start + step_cols
        block = square[start:, start:finish]
        if start > 0:
            left = result[start:, :start]
            block = block - lax.dot_general(
                left,
                left[:step_cols],
                contract,
                precision=lax.Precision.HIGHEST,
                preferred_element_type=jnp.float32,
            )
        diag_factor = jnp.linalg.cholesky(block[:step_cols])
        if finish < size_total:
            below = solve_rows(diag_factor, block[step_cols:])
            column_part = jnp.concatenate([diag_factor, below], 0)
        else:
            column_part = diag_factor
        result = result.at[start:, start:finish].set(column_part)
    return result


def body(kernel):
    tile_size = TILE
    rows_local, cols_local = kernel.shape
    row_count = lax.axis_size("row")
    col_count = lax.axis_size("col")
    row_index = lax.axis_index("row")
    col_index = lax.axis_index("col")
    row_tile = (row_index + row_count * (jnp.arange(rows_local) // tile_size))[:, None]
    col_tile = (col_index + col_count * (jnp.arange(cols_local) // tile_size))[None, :]
    highest = lax.Precision.HIGHEST
    contract = (((1,), (1,)), ((), ()))
    matrix = kernel
    leading = kernel
    for panel_index in range(2):
        first_tile = 2 * panel_index
        second = first_tile + 1
        pieces = []
        for owner_tile in (first_tile, second):
            pieces.append(broadcast(leading, "col", owner_tile))
        columns = jnp.concatenate(pieces, 1)
        corners = []
        for owner_tile in (first_tile, second):
            start_row = owner_tile // row_count * tile_size
            corners.append(
                broadcast(columns[start_row : start_row + tile_size], "row", owner_tile % row_count)
            )
        corner = jnp.concatenate(corners, 0)
        factor = factor_blocks(corner)
        solved = solve_rows(factor, columns)
        combined = jnp.where(row_tile > second, solved, 0.0)
        for owner_tile in (first_tile, second):
            start_row = owner_tile // row_count * tile_size
            offset = (owner_tile - first_tile) * tile_size
            current = combined[start_row : start_row + tile_size]
            chosen = jnp.where(
                row_index == owner_tile % row_count, factor[offset : offset + tile_size], current
            )
            combined = combined.at[start_row : start_row + tile_size].set(chosen)
        lower = jnp.where(row_tile > second, combined, 0.0)
        base_tile = col_index // row_count
        selected = lax.dynamic_slice_in_dim(lower, (base_tile + 0) * tile_size, tile_size, 0)
        across = broadcast(selected, "row", col_index % row_count)
        updated = matrix - lax.dot_general(
            lower, across, contract, precision=highest, preferred_element_type=jnp.float32
        )
        head_block = updated
        rest_block = updated[:, tile_size:]
        head_block = jnp.where(
            col_index == first_tile,
            combined[:, :tile_size],
            jnp.where(col_index == second, combined[:, tile_size:], head_block),
        )
        band_rows = (row_tile == first_tile) | (row_tile == second)
        head_block = jnp.where(band_rows & (col_tile > second), 0.0, head_block)
        rest_block = jnp.where(band_rows & (col_tile[:, tile_size:] > second), 0.0, rest_block)
        leading = head_block
        matrix = jnp.concatenate([head_block, rest_block], 1)
    return matrix


def solution(mesh):
    return jax.shard_map(
        body,
        mesh=mesh,
        in_specs=(P("row", "col"),),
        out_specs=P("row", "col"),
        check_vma=False,
    )
```

profile of v0, /device:TPU:101, one launch (start us, length us, event | category | flops | bytes accessed | tf_op | source)
XLA Modules:
  0.0 1333.5 jit_solution(8388380659919746788)
XLA Ops:
  10.9 104.8 %all-reduce.19.cloned.1.call-done = (f32[1024,512]{1,0:T(8,128)}, f32[1024,512]{1,0:T(8,128)}) async-done(((f32[1024,512]{1,0:T(8,128)}, f32[1024,512]{1,0:T(8,128)}), (f32[1024,512]{1,0:T(8,128)}, f32[1024,512]{1,0:T(8,128)})) %all-reduce.19.cloned.1.call-update) | async-done | bytes 4194320 | tf_op jit(solution)/shard_map/psum | solution.py:11
  123.5 71.6 %all-reduce.23.cloned.1.call-done = (f32[512,1024]{1,0:T(8,128)}, f32[512,1024]{1,0:T(8,128)}) async-done(((f32[512,1024]{1,0:T(8,128)}, f32[512,1024]{1,0:T(8,128)}), (f32[512,1024]{1,0:T(8,128)}, f32[512,1024]{1,0:T(8,128)})) %all-reduce.23.cloned.1.call-update) | async-done | bytes 4194320 | tf_op jit(solution)/shard_map/psum | solution.py:11
  200.3 11.7 cholesky.254
  213.4 9.8 custom-call.34
  228.7 11.7 cholesky.265
  241.8 9.9 custom-call.35
  256.8 11.7 cholesky.276
  269.9 9.8 custom-call.36
  283.5 11.9 cholesky.287
  296.8 9.8 custom-call.37
  310.2 11.7 cholesky.298
  323.3 10.2 custom-call.38
  337.0 11.7 cholesky.309
  350.1 9.8 custom-call.39
  363.1 11.9 cholesky.320
  376.3 9.8 custom-call.40
  389.0 11.7 cholesky.331
  407.5 23.9 %while.24 = (s32[]{:T(128)}, f32[1024,1024]{1,0:T(8,128)}, s32[8,2]{0,1:T(2,128)S(1)}, f32[8,128,128]{2,1,0:T(8,128)S(1)}, s32[]{:T(128)}) while((s32[]{:T(128)}, f32[1024,1024]{1,0:T(8,128)}, s32[8,2]{0,1:T(2,128)S(1)}, f32[8,128,128]{2,1,0:T(8,128)S(1)}, s32[]{:T(128)}) %tuple.178), condition=%wide.while_cond.20, body=%wide.while_body.20.sunk | while | flops 2 | bytes 131181 | solution.py:15
  431.4 78.8 %custom-call.41 = f32[8,128,128]{1,2,0:T(8,128)S(1)} custom-call(f32[8,128,128]{2,1,0:T(8,128)S(1)} %get-tuple-element.268), custom_call_target="InvertDiagBlocksLowerTriangular" | custom-call | tf_op jit(solution)/shard_map/jit(_solve_triangular)/triangular_solve | solution.py:15
  537.6 6.3 convolution_subtract_fusion.5
  546.6 7.2 convolution_subtract_fusion.3
  556.1 8.4 convolution_subtract_fusion.8
  581.9 65.5 %all-reduce.13.cloned.1.call-done = f32[512,1024]{1,0:T(8,128)} async-done(((f32[512,1024]{1,0:T(8,128)}), f32[512,1024]{1,0:T(8,128)}) %all-reduce.13.cloned.1.call-update) | async-done | bytes 2097168 | tf_op jit(solution)/shard_map/psum | solution.py:11
  647.4 12.5 broadcast_select_fusion.4
  660.0 104.1 %all-reduce.17.cloned.1.call-done = (f32[1024,512]{1,0:T(8,128)}, f32[1024,512]{1,0:T(8,128)}) async-done(((f32[1024,512]{1,0:T(8,128)}, f32[1024,512]{1,0:T(8,128)}), (f32[1024,512]{1,0:T(8,128)}, f32[1024,512]{1,0:T(8,128)})) %all-reduce.17.cloned.1.call-update) | async-done | bytes 4194320 | tf_op jit(solution)/shard_map/psum | solution.py:11
  777.1 72.0 %all-reduce.21.cloned.1.call-done = (f32[512,1024]{0,1:T(8,128)}, f32[512,1024]{0,1:T(8,128)}) async-done(((f32[512,1024]{0,1:T(8,128)}, f32[512,1024]{0,1:T(8,128)}), (f32[512,1024]{0,1:T(8,128)}, f32[512,1024]{0,1:T(8,128)})) %all-reduce.21.cloned.1.call-update) | async-done | bytes 4194320 | tf_op jit(solution)/shard_map/psum | solution.py:11
  854.2 11.7 cholesky.342
  867.2 9.8 custom-call.42
  883.0 11.7 cholesky.353
  896.1 9.9 custom-call.43
  911.4 11.7 cholesky.364
  924.5 9.8 custom-call.44
  938.6 11.9 cholesky.375
  951.8 9.8 custom-call.45
  965.6 11.7 cholesky.386
  978.7 10.2 custom-call.46
  992.6 11.7 cholesky.397
  1005.7 9.8 custom-call.47
  1018.9 11.8 cholesky.408
  1032.1 9.8 custom-call.48
  1044.7 11.7 cholesky.419
  1063.2 23.1 %while.25 = (s32[]{:T(128)}, f32[1024,1024]{1,0:T(8,128)}, s32[8,2]{0,1:T(2,128)S(1)}, f32[8,128,128]{2,1,0:T(8,128)S(1)}, s32[]{:T(128)}) while((s32[]{:T(128)}, f32[1024,1024]{1,0:T(8,128)}, s32[8,2]{0,1:T(2,128)S(1)}, f32[8,128,128]{2,1,0:T(8,128)S(1)}, s32[]{:T(128)}) %tuple.200), condition=%wide.while_cond.20.clone, body=%wide.while_body.20.clone.sunk | while | flops 2 | bytes 131181 | solution.py:15
  1086.2 78.8 %custom-call.49 = f32[8,128,128]{1,2,0:T(8,128)S(1)} custom-call(f32[8,128,128]{2,1,0:T(8,128)S(1)} %get-tuple-element.269), custom_call_target="InvertDiagBlocksLowerTriangular" | custom-call | tf_op jit(solution)/shard_map/jit(_solve_triangular)/triangular_solve | solution.py:15
  1192.5 6.3 convolution_subtract_fusion.4
  1201.5 7.2 convolution_subtract_fusion.2
  1210.9 8.4 convolution_subtract_fusion.6
  1248.2 65.5 %all-reduce.15.cloned.1.call-done = f32[512,1024]{0,1:T(8,128)} async-done(((f32[512,1024]{0,1:T(8,128)}), f32[512,1024]{0,1:T(8,128)}) %all-reduce.15.cloned.1.call-update) | async-done | bytes 2097168 | tf_op jit(solution)/shard_map/psum | solution.py:11
  1313.7 12.7 fusion.3
  (344 shorter events, 281.5 us)
Async XLA Ops:
  6.5 109.2 %all-reduce.19.cloned.1.call-start = ((), (), s32[]{:S(2)}) async-start(), calls=%async_computation.3 | async-start | bytes 8388608 | tf_op jit(solution)/shard_map/psum | solution.py:11
  10.8 184.3 %all-reduce.23.cloned.1.call-start = ((), (), s32[]{:S(2)}) async-start(), calls=%async_computation.5 | async-start | bytes 8388608 | tf_op jit(solution)/shard_map/psum | solution.py:11
  115.7 2.2 copy-start.13
  118.1 1.9 copy-start.7
  122.6 524.8 %all-reduce.13.cloned.1.call-start = ((), (), s32[]{:S(2)}) async-start(), calls=%async_computation | async-start | bytes 4194304 | tf_op jit(solution)/shard_map/psum | solution.py:11
  195.1 28.1 %copy-start.11 = (f32[512,1024]{1,0:T(8,128)S(1)}, f32[512,1024]{1,0:T(8,128)}, u32[]{:S(2)}) copy-start(f32[512,1024]{1,0:T(8,128)} %get-tuple-element.293) | copy-start | bytes 6291460
  252.8 2.0 copy-start
  510.2 15.7 %copy-start.21 = (f32[8,128,128]{1,2,0:T(8,128)}, f32[8,128,128]{1,2,0:T(8,128)S(1)}, u32[]{:S(2)}) copy-start(f32[8,128,128]{1,2,0:T(8,128)S(1)} %custom-call.41) | copy-start | bytes 1572868
  565.4 5.4 copy-start.15
  569.6 1.0 copy-start.19
  569.6 1.2 copy-start.17
  572.7 2.2 copy-start.1
  576.4 2.0 copy-start.4
  578.4 1.9 copy-start.5
  580.3 67.1 %copy-start.9 = (f32[1024,512]{1,0:T(8,128)S(1)}, f32[1024,512]{1,0:T(8,128)}, u32[]{:S(2)}) copy-start(f32[1024,512]{1,0:T(8,128)} %param.58) | copy-start | bytes 6291460
  581.9 182.3 %all-reduce.17.cloned.1.call-start = ((), (), s32[]{:S(2)}) async-start(), calls=%async_computation.2 | async-start | bytes 8388608 | tf_op jit(solution)/shard_map/psum | solution.py:11
  659.9 189.2 %all-reduce.21.cloned.1.call-start = ((), (), s32[]{:S(2)}) async-start(), calls=%async_computation.4 | async-start | bytes 8388608 | tf_op jit(solution)/shard_map/psum | solution.py:11
  764.1 2.2 copy-start.14
  766.5 1.9 copy-start.8
  776.6 537.1 %all-reduce.15.cloned.1.call-start = ((), (), s32[]{:S(2)}) async-start(), calls=%async_computation.1 | async-start | bytes 4194304 | tf_op jit(solution)/shard_map/psum | solution.py:11
  849.1 27.9 %copy-start.12 = (f32[512,1024]{0,1:T(8,128)S(1)}, f32[512,1024]{0,1:T(8,128)}, u32[]{:S(2)}) copy-start(f32[512,1024]{0,1:T(8,128)} %get-tuple-element.291) | copy-start | bytes 6291460
  907.4 2.0 copy-start.2
  1165.0 15.7 %copy-start.22 = (f32[8,128,128]{1,2,0:T(8,128)}, f32[8,128,128]{1,2,0:T(8,128)S(1)}, u32[]{:S(2)}) copy-start(f32[8,128,128]{1,2,0:T(8,128)S(1)} %custom-call.49) | copy-start | bytes 1572868
  1220.3 5.4 copy-start.16
  1224.4 1.0 copy-start.20
  1224.4 1.2 copy-start.18
  1227.5 3.7 copy-start.3
  1244.5 1.9 copy-start.6
  1246.5 67.2 %copy-start.10 = (f32[1024,512]{1,0:T(8,128)S(1)}, f32[1024,512]{1,0:T(8,128)}, u32[]{:S(2)}) copy-start(f32[1024,512]{1,0:T(8,128)} %get-tuple-element.376) | copy-start | bytes 6291460
Sparse Core Ops, SparseCore 0:
  10.9 104.7 all-reduce.18
  122.8 72.2 all-reduce.22
  582.0 65.3 all-reduce.12
  660.0 104.0 all-reduce.16
  776.8 72.2 all-reduce.20
  1248.3 65.3 all-reduce.14
where the time goes:
time: 1350 us; the launch traced here: 1330 us
  other arithmetic  552 us (41%)
  waiting for transfers between devices  484 us (36%)
  matrix products  172 us (13%)
  local copies, waits for them, and re-layouts  110 us (8%)
  between operations  15.2 us (1%)
    psum x6, waiting for transfers between devices, broadcast(): return lax.psum(jnp.where(mine, x, jnp.zeros_like(x)), axis)  484 us
    another operation x33, other arithmetic, solve_rows(): return jax.scipy.linalg.solve_triangular(factor, values.T, lower=True).T  315 us
    another operation x48, other arithmetic, factor_blocks(): diag_factor = jnp.linalg.cholesky(block[:step_cols])  199 us
    another operation x44, matrix products, solve_rows(): return jax.scipy.linalg.solve_triangular(factor, values.T, lower=True).T  118 us
    another operation x65, local copies, waits for them, and re-layouts, solve_rows(): return jax.scipy.linalg.solve_triangular(factor, values.T, lower=True).T  58.5 us
    unnamed x66, local copies, waits for them, and re-layouts  32.4 us
    dot_general x14, matrix products, factor_blocks(): lax.dot_general(left, left[:step_cols], contract, precision=lax.Precision...  28.8 us
  transfers between devices with their start and end apart: 6, of which 6 were waited for; matrix products, arithmetic and copies ran while one was open for 0% of the time, Pallas kernels for 0%

commit v1 on v0

v1 whole, which is shorter than its diff:
```python
import functools

import jax
import jax.numpy as jnp
from jax import lax
from jax.experimental import pallas as pl
from jax.experimental.pallas import tpu as pltpu
from jax.sharding import PartitionSpec as P

T = 512
W = 1024
B = 128
H = 256
MESH = pl.DeviceIdType.MESH
NT = (((1,), (1,)), ((), ()))
NN = (((1,), (0,)), ((), ()))


def split(x):
    hi = x.astype(jnp.bfloat16)
    lo = (x - hi.astype(jnp.float32)).astype(jnp.bfloat16)
    return hi, lo


def dot3(a, b, dims=NT):
    (ah, al), (bh, bl) = a, b
    d = functools.partial(
        lax.dot_general, dimension_numbers=dims, preferred_element_type=jnp.float32
    )
    return d(ah, bh) + (d(ah, bl) + d(al, bh))


def lane(x, i):
    return jnp.broadcast_to(x[:, i : i + 1], (8, B))


def sub(x, i):
    return jnp.broadcast_to(x[i : i + 1, :], (8, B))


def chol_block(block):
    n = B // 8
    li = lax.broadcasted_iota(jnp.int32, (8, B), 1)
    si = lax.broadcasted_iota(jnp.int32, (8, B), 0)
    rows = [block[8 * i : 8 * i + 8] for i in range(n)]
    eye = [(li == si + 8 * i).astype(jnp.float32) for i in range(n)]
    upper, inverse = [], []

    def merge(xs):
        out = xs[0]
        for t in range(1, 8):
            out = jnp.where(si == t, xs[t], out)
        return out

    for j in range(n):
        o = 8 * j
        cols = [lane(rows[j], o + q) for q in range(8)]
        m = {(p, q): sub(cols[q], p) for q in range(8) for p in range(q, 8)}
        rb = [sub(rows[j], p) for p in range(8)]
        eb = [sub(eye[j], p) for p in range(8)]
        nxt = j + 1 < n
        if nxt:
            raw = [[lane(rows[i], o + q) for q in range(8)] for i in range(j + 1, n)]
            nc = list(raw[0])
        rk = [None] * 8
        fs = {}
        for k in range(8):
            rk[k] = 1.0 / m[k, k]
            for q in range(k + 1, 8):
                if q == k + 1:
                    m[q, q] = m[q, q] - (m[q, k] * m[q, k]) * rk[k]
                f = m[q, k] * rk[k]
                fs[q, k] = f
                for p in range(q + (1 if q == k + 1 else 0), 8):
                    m[p, q] = m[p, q] - m[p, k] * f
                rb[q] = rb[q] - f * rb[k]
                eb[q] = eb[q] - f * eb[k]
                if nxt:
                    nc[q] = nc[q] - f * nc[k]
            if nxt:
                c = nc[k] * rk[k]
                rows[j + 1] = rows[j + 1] - c * rb[k]
                eye[j + 1] = eye[j + 1] - c * eb[k]
        sk = lax.rsqrt(merge([m[k, k] for k in range(8)]))
        upper.append(merge(rb) * sk)
        inverse.append(merge(eb) * sk)
        if j + 2 < n:
            vr = [rb[k] * rk[k] for k in range(8)]
            ve = [eb[k] * rk[k] for k in range(8)]
            for q in range(7, -1, -1):
                for k in range(q):
                    vr[k] = vr[k] - fs[q, k] * vr[q]
                    ve[k] = ve[k] - fs[q, k] * ve[q]
            for i in range(j + 2, n):
                ar, ae = rows[i], eye[i]
                for q in range(8):
                    c = raw[i - j - 1][q]
                    ar = ar - c * vr[q]
                    ae = ae - c * ve[q]
                rows[i], eye[i] = ar, ae
    return jnp.concatenate(upper, 0), jnp.concatenate(inverse, 0)


def body(
    a_ref, m_ref, rbuf, cbuf, dbuf, lref, wref, lh, ll, wh, wl, xh, xl, uh, ul,
    ssem, r1, r2, r3, c1, c2, c3, d1, d2, d3, d4, d5, lsem,
):
    row = lax.axis_index("row")
    col = lax.axis_index("col")
    h = lax.rem(row, 2)
    z = lax.div(row, 2)
    x = lax.div(col, 4)
    y = lax.rem(col, 4)
    major = jnp.where(h == 0, x, y)
    minor = jnp.where(h == 0, y, x)
    mine = 4 * major + minor

    def col_of(ma, mi):
        return jnp.where(h == 0, 4 * ma + mi, 4 * mi + ma)

    def put(src, dst, send, recv, row_to, col_to):
        return pltpu.make_async_remote_copy(
            src_ref=src, dst_ref=dst, send_sem=send, recv_sem=recv,
            device_id=(row_to, col_to), device_id_type=MESH,
        )

    barrier = pltpu.get_barrier_semaphore()

    @pl.loop(1, 16)
    def _(t):
        pl.semaphore_signal(
            barrier, inc=1, device_id=(row, lax.rem(col + t, 16)), device_id_type=MESH
        )

    for t in range(1, 4):
        pl.semaphore_signal(
            barrier, inc=1, device_id=(2 * lax.rem(z + t, 4) + h, col), device_id_type=MESH
        )
    pl.semaphore_signal(barrier, inc=1, device_id=(2 * z + 1 - h, col), device_id_type=MESH)
    m_ref[...] = a_ref[...]
    pl.semaphore_wait(barrier, 19)

    def panel(p):
        first = 2 * p
        second = first + 1
        is_source = (x == 0) & ((y == first) | (y == second))
        half = jnp.where(y == second, 1, 0)
        mycols = pl.ds(pl.multiple_of(half * T, T), T)
        scols = [pl.ds(0, T), pl.ds(T, T)]
        R, C, D = rbuf.at[p], cbuf.at[p], dbuf.at[p]

        def rows(start, size):
            return pl.ds(pl.multiple_of(start * size, size), size)

        def d_rows(i, size):
            return pl.ds(pl.multiple_of(h * T + i * size, size), size)

        d_source = is_source & (z == p) & (half <= h)

        def d_scatter(i):
            return put(
                m_ref.at[rows(i, 32), :], D.at[d_rows(i, 32), mycols],
                ssem.at[p, 0, i], d1.at[p, half], row, col_of(lax.div(i, 4), lax.rem(i, 4)),
            )

        @pl.when(d_source)
        def _():
            @pl.loop(0, 16)
            def _(i):
                @pl.when(i != mine)
                def _():
                    d_scatter(i).start()

            own = pltpu.make_async_copy(
                m_ref.at[rows(mine, 32), :], D.at[d_rows(mine, 32), mycols], lsem.at[p, 0]
            )
            own.start()
            own.wait()

        def each_tile(cond, fn):
            for s in range(2):
                @pl.when(cond & (h >= s))
                def _():
                    fn(s)

        def d_from(s):
            put(
                m_ref.at[rows(mine, 32), :], D.at[d_rows(mine, 32), scols[s]],
                ssem.at[p, 0, 0], d1.at[p, s], row, col,
            ).wait_recv()

        for s in range(2):
            @pl.when((z == p) & (h >= s) & jnp.logical_not((x == 0) & (y == first + s)))
            def _():
                d_from(s)

        def d_z(s, t):
            ref = D.at[d_rows(mine, 32), scols[s]]
            return put(
                ref, ref, ssem.at[p, 1, s * 3 + t - 1], d2.at[p, s], 2 * lax.rem(z + t, 4) + h, col
            )

        def d_minor(s, t):
            ref = D.at[d_rows(mine, 32), scols[s]]
            return put(
                ref, ref, ssem.at[p, 2, s * 3 + t - 1], d3.at[p, s * 3 + t - 1],
                row, col_of(major, lax.rem(minor + t, 4)),
            )

        def d_minor_in(s, t):
            ref = D.at[d_rows(4 * major + lax.rem(minor + 4 - t, 4), 32), scols[s]]
            put(ref, ref, ssem.at[p, 2, 0], d3.at[p, s * 3 + t - 1], row, col).wait_recv()

        def d_major(s, t):
            ref = D.at[d_rows(major, 128), scols[s]]
            return put(
                ref, ref, ssem.at[p, 3, s * 3 + t - 1], d4.at[p, s * 3 + t - 1],
                row, col_of(lax.rem(major + t, 4), minor),
            )

        def d_major_in(s, t):
            ref = D.at[d_rows(lax.rem(major + 4 - t, 4), 128), scols[s]]
            put(ref, ref, ssem.at[p, 3, 0], d4.at[p, s * 3 + t - 1], row, col).wait_recv()

        def d_core(s):
            ref = D.at[pl.ds(pl.multiple_of(h * T, T), T), scols[s]]
            return put(ref, ref, ssem.at[p, 4, s], d5.at[p, s], 2 * z + 1 - h, col)

        def d_core_in(s):
            ref = D.at[pl.ds(pl.multiple_of((1 - h) * T, T), T), scols[s]]
            put(ref, ref, ssem.at[p, 4, 0], d5.at[p, s], row, col).wait_recv()

        each_tile(z == p, lambda s: [d_z(s, t).start() for t in (1, 2, 3)])
        each_tile(z != p, lambda s: d_z(s, 1).wait_recv())
        each_tile(z >= 0, lambda s: [d_minor(s, t).start() for t in (1, 2, 3)])
        each_tile(z >= 0, lambda s: [d_minor_in(s, t) for t in (1, 2, 3)])
        each_tile(z >= 0, lambda s: [d_major(s, t).start() for t in (1, 2, 3)])
        each_tile(z >= 0, lambda s: [d_major_in(s, t) for t in (1, 2, 3)])
        each_tile(z >= 0, lambda s: d_core(s).start())
        for s in range(2):
            @pl.when(1 - h >= s)
            def _():
                d_core_in(s)

        def r_scatter(i):
            return put(
                m_ref.at[rows(i, 64), :], R.at[rows(i, 64), mycols],
                ssem.at[p, 5, i], r1.at[p, half], row, col_of(lax.div(i, 4), lax.rem(i, 4)),
            )

        def r_minor(t):
            ref = R.at[rows(mine, 64), :]
            return put(
                ref, ref, ssem.at[p, 6, t - 1], r2.at[p, t - 1],
                row, col_of(major, lax.rem(minor + t, 4)),
            )

        def r_minor_in(t):
            ref = R.at[rows(4 * major + lax.rem(minor + 4 - t, 4), 64), :]
            put(ref, ref, ssem.at[p, 6, 0], r2.at[p, t - 1], row, col).wait_recv()

        def r_major(t):
            ref = R.at[rows(major, 256), :]
            return put(
                ref, ref, ssem.at[p, 7, t - 1], r3.at[p, t - 1],
                row, col_of(lax.rem(major + t, 4), minor),
            )

        def r_major_in(t):
            ref = R.at[rows(lax.rem(major + 4 - t, 4), 256), :]
            put(ref, ref, ssem.at[p, 7, 0], r3.at[p, t - 1], row, col).wait_recv()

        def c_rows(q):
            return pl.ds(pl.multiple_of(h * T + q * B, B), B)

        def c_first(t, which):
            zt = lax.rem(z + t, 4)
            q = zt if which == 0 else z
            return put(
                m_ref.at[rows(q, B), :], C.at[c_rows(q), :],
                ssem.at[p, 8, 2 * (t - 1) + which], c1.at[p, which], 2 * zt + h, col,
            )

        def c_first_in(which):
            q = z if which == 0 else p
            ref = C.at[c_rows(q), :]
            put(ref, ref, ssem.at[p, 8, 0], c1.at[p, which], row, col).wait_recv()

        def c_second(t):
            ref = C.at[c_rows(z), :]
            return put(
                ref, ref, ssem.at[p, 9, t - 1], c2.at[p, t - 1], 2 * lax.rem(z + t, 4) + h, col
            )

        def c_second_in(t):
            ref = C.at[c_rows(lax.rem(z + 4 - t, 4)), :]
            put(ref, ref, ssem.at[p, 9, 0], c2.at[p, t - 1], row, col).wait_recv()

        def c_core():
            ref = C.at[pl.ds(pl.multiple_of(h * T, T), T), :]
            return put(ref, ref, ssem.at[p, 10, 0], c3.at[p, 0], 2 * z + 1 - h, col)

        def c_core_in():
            ref = C.at[pl.ds(pl.multiple_of((1 - h) * T, T), T), :]
            put(ref, ref, ssem.at[p, 10, 0], c3.at[p, 0], row, col).wait_recv()

        def stage0():
            @pl.when(is_source)
            def _():
                @pl.loop(0, 16)
                def _(i):
                    @pl.when(i != mine)
                    def _():
                        r_scatter(i).start()

                own = pltpu.make_async_copy(
                    m_ref.at[rows(mine, 64), :], R.at[rows(mine, 64), mycols], lsem.at[p, 1]
                )
                own.start()
                own.wait()

            @pl.when(z == p)
            def _():
                for t in (1, 2, 3):
                    for which in (0, 1):
                        c_first(t, which).start()
                own = pltpu.make_async_copy(
                    m_ref.at[pl.ds(0, T), :],
                    C.at[pl.ds(pl.multiple_of(h * T, T), T), :], lsem.at[p, 2],
                )
                own.start()
                own.wait()

        def stage1():
            for s in range(2):
                @pl.when(jnp.logical_not((x == 0) & (y == first + s)))
                def _():
                    put(
                        m_ref.at[rows(mine, 64), :], R.at[rows(mine, 64), scols[s]],
                        ssem.at[p, 5, 0], r1.at[p, s], row, col,
                    ).wait_recv()
            for t in (1, 2, 3):
                r_minor(t).start()

            @pl.when(z != p)
            def _():
                c_first_in(0)
                for t in (1, 2, 3):
                    @pl.when(lax.rem(z + t, 4) != p)
                    def _():
                        c_second(t).start()
                c_first_in(1)

        def stage2():
            for t in (1, 2, 3):
                r_minor_in(t)
            for t in (1, 2, 3):
                r_major(t).start()

            @pl.when(z != p)
            def _():
                for t in (1, 2, 3):
                    @pl.when(lax.rem(z + 4 - t, 4) != p)
                    def _():
                        c_second_in(t)

            c_core().start()

        def stage3():
            for t in (1, 2, 3):
                r_major_in(t)
            c_core_in()

        def drain_d():
            @pl.when(d_source)
            def _():
                @pl.loop(0, 16)
                def _(i):
                    @pl.when(i != mine)
                    def _():
                        d_scatter(i).wait_send()

            each_tile(z == p, lambda s: [d_z(s, t).wait_send() for t in (1, 2, 3)])
            each_tile(z >= 0, lambda s: [d_minor(s, t).wait_send() for t in (1, 2, 3)])
            each_tile(z >= 0, lambda s: [d_major(s, t).wait_send() for t in (1, 2, 3)])
            each_tile(z >= 0, lambda s: d_core(s).wait_send())

        def drain_rc():
            @pl.when(is_source)
            def _():
                @pl.loop(0, 16)
                def _(i):
                    @pl.when(i != mine)
                    def _():
                        r_scatter(i).wait_send()

            for t in (1, 2, 3):
                r_minor(t).wait_send()
                r_major(t).wait_send()

            @pl.when(z == p)
            def _():
                for t in (1, 2, 3):
                    for which in (0, 1):
                        c_first(t, which).wait_send()

            @pl.when(z != p)
            def _():
                for t in (1, 2, 3):
                    @pl.when(lax.rem(z + t, 4) != p)
                    def _():
                        c_second(t).wait_send()

            c_core().wait_send()

        stage0()
        drain_d()

        lref[...] = jnp.zeros_like(lref)
        nb = W // B

        @pl.loop(0, nb)
        def _(k):
            o = pl.multiple_of(k * B, B)

            @pl.when(k == 1)
            def _():
                stage1()

            @pl.when(k == 3)
            def _():
                stage2()

            upper, inverse = chol_block(D[pl.ds(o, B), pl.ds(o, B)])
            wref[pl.ds(o, B), :] = inverse
            ri = lax.broadcasted_iota(jnp.int32, (B, B), 0)
            ci = lax.broadcasted_iota(jnp.int32, (B, B), 1)
            lref[pl.ds(o, B), pl.ds(o, B)] = jnp.where(ri >= ci, upper.T, 0.0)
            for kk in range(nb - 1):
                @pl.when(k == kk)
                def _():
                    s, e = kk * B, kk * B + B
                    xk = dot3(split(D[e:, s:e]), split(inverse))
                    lref[e:, s:e] = xk
                    xs = split(xk)
                    for c0 in range(e, W, H):
                        c1_ = min(c0 + H, W)
                        left = (xs[0][c0 - e :], xs[1][c0 - e :])
                        right = (xs[0][c0 - e : c1_ - e], xs[1][c0 - e : c1_ - e])
                        D[c0:, c0:c1_] = D[c0:, c0:c1_] - dot3(left, right)

        for g in range(4):
            w0 = wref[g * H : g * H + B, :]
            w1 = wref[g * H + B : g * H + H, :]
            l10 = lref[g * H + B : g * H + H, g * H : g * H + B]
            low = dot3(split(w1), split(dot3(split(l10), split(w0), NN)), NN)
            big = jnp.concatenate(
                [
                    jnp.concatenate([w0, jnp.zeros_like(w0)], 1),
                    jnp.concatenate([-low, w1], 1),
                ],
                0,
            )
            wh[g], wl[g] = split(big)

        @pl.loop(0, 4)
        def _(g):
            rs = rows(g, H)
            a, b = split(lref[rs, :])
            lh[rs, :] = a
            ll[rs, :] = b

        stage3()
        drain_rc()

        @pl.loop(0, 4)
        def _(g):
            rs = rows(g, H)
            for kb in range(4):
                ks = pl.ds(kb * H, H)
                xk = dot3(split(R[rs, ks]), (wh[kb], wl[kb]))
                R[rs, ks] = xk
                xs = split(xk)
                xh[rs, ks], xl[rs, ks] = xs
                for jb in range(kb + 1, 4):
                    js = pl.ds(jb * H, H)
                    R[rs, js] = R[rs, js] - dot3(xs, (lh[js, ks], ll[js, ks]))

        @pl.loop(0, 2)
        def _(g):
            cs = rows(g, H)
            for kb in range(4):
                ks = pl.ds(kb * H, H)
                us = split(dot3((wh[kb], wl[kb]), split(C[ks, cs]), NN))
                uh[ks, cs], ul[ks, cs] = us
                for jb in range(kb + 1, 4):
                    js = pl.ds(jb * H, H)
                    C[js, cs] = C[js, cs] - dot3((lh[js, ks], ll[js, ks]), us, NN)

        right_of = col > second
        in_panel = (col == first) | (col == second)
        top_below = row > second
        top_band = (row == first) | (row == second)

        def update(g):
            rs = rows(g, H)
            for n in range(2):
                cs = pl.ds(n * H, H)
                m_ref[rs, cs] = m_ref[rs, cs] - dot3(
                    (xh[rs, :], xl[rs, :]), (uh[:, cs], ul[:, cs]), NN
                )

        pcols = pl.ds(pl.multiple_of(jnp.where(col == second, T, 0), T), T)

        @pl.when(right_of)
        def _():
            @pl.when(top_below)
            def _():
                pl.loop(0, 2)(update)

            @pl.when(top_band)
            def _():
                m_ref[0:T, :] = jnp.zeros((T, T), jnp.float32)

            pl.loop(2, 4)(update)

        @pl.when(in_panel)
        def _():
            @pl.when(top_below)
            def _():
                m_ref[0:T, :] = R[0:T, pcols]

            @pl.when(top_band)
            def _():
                band = pl.ds(pl.multiple_of(jnp.where(row == second, T, 0), T), T)
                m_ref[0:T, :] = lref[band, pcols]

            m_ref[T : 2 * T, :] = R[T : 2 * T, pcols]

    pl.loop(0, 2)(panel)


def local(kernel):
    f32, b16 = jnp.float32, jnp.bfloat16
    dma = pltpu.SemaphoreType.DMA
    return pl.pallas_call(
        body,
        out_shape=jax.ShapeDtypeStruct((W, T), f32),
        in_specs=[pl.BlockSpec(memory_space=pltpu.VMEM)],
        out_specs=pl.BlockSpec(memory_space=pltpu.VMEM),
        scratch_shapes=[
            pltpu.VMEM((2, W, W), f32),
            pltpu.VMEM((2, W, T), f32),
            pltpu.VMEM((2, W, W), f32),
            pltpu.VMEM((W, W), f32),
            pltpu.VMEM((W, B), f32),
            pltpu.VMEM((W, W), b16),
            pltpu.VMEM((W, W), b16),
            pltpu.VMEM((4, H, H), b16),
            pltpu.VMEM((4, H, H), b16),
            pltpu.VMEM((W, W), b16),
            pltpu.VMEM((W, W), b16),
            pltpu.VMEM((W, T), b16),
            pltpu.VMEM((W, T), b16),
            dma((2, 11, 16)),
            dma((2, 2)), dma((2, 3)), dma((2, 3)),
            dma((2, 2)), dma((2, 3)), dma((2, 1)),
            dma((2, 2)), dma((2, 2)), dma((2, 6)), dma((2, 6)), dma((2, 2)),
            dma((2, 3)),
        ],
        compiler_params=pltpu.CompilerParams(
            collective_id=0, has_side_effects=True, vmem_limit_bytes=60 * 1024 * 1024
        ),
        cost_estimate=pl.CostEstimate(
            flops=20_000_000_000, bytes_accessed=8_000_000, transcendentals=0
        ),
        name="two_panels",
    )(kernel)


def solution(mesh):
    return jax.shard_map(
        local,
        mesh=mesh,
        in_specs=(P("row", "col"),),
        out_specs=P("row", "col"),
        check_vma=False,
    )
```

time: 1350 us -> 249 us (0.18)
  other arithmetic: 552 us -> 0 us
  waiting for transfers between devices: 484 us -> 0 us
  Pallas kernels: 0 us -> 241 us
  matrix products: 172 us -> 0 us
  local copies, waits for them, and re-layouts: 110 us -> 3.08 us
  between operations: 15.2 us -> 0.01 us
    another operation x84 -> x0, other arithmetic: 516 us -> none  [the longest x33 315 us: solve_rows(): return jax.scipy.linalg.solve_triangular(factor, values.T, lower=True).T]
    psum x6 -> x0, waiting for transfers between devices: 484 us -> none  [broadcast(): return lax.psum(jnp.where(mine, x, jnp.zeros_like(x)), axis)]
    pallas_call x0 -> x1, Pallas kernels: none -> 241 us  [local(): pl.pallas_call(body, out_shape=jax.ShapeDtypeStruct((W, T), f32), in_spec...]
    another operation x44 -> x0, matrix products: 118 us -> none  [solve_rows(): return jax.scipy.linalg.solve_triangular(factor, values.T, lower=True).T]
    another operation x65 -> x0, local copies, waits for them, and re-layouts: 58.5 us -> none  [solve_rows(): return jax.scipy.linalg.solve_triangular(factor, values.T, lower=True).T]
    dot_general x16 -> x0, matrix products: 54 us -> none  [the longest x14 28.8 us: factor_blocks(): lax.dot_general(left, left[:step_cols], contract, precision=lax.Precision...]
    unnamed x66 -> x1, local copies, waits for them, and re-layouts: 32.4 us -> 3.08 us
    scatter x18 -> x0, other arithmetic: 17.1 us -> none  [the longest x14 10.2 us: factor_blocks(): result = result.at[start:, start:finish].set(column_part)]
  transfers between devices with their start and end apart: 6 -> 0, of which waited for: 6 -> 0; matrix products, arithmetic and copies ran while one was open for 0% -> 0% of each run, Pallas kernels for 0% -> 0%
where the time goes in v1:
time: 249 us; the launch traced here: 244 us
  Pallas kernels  241 us (97%)
  local copies, waits for them, and re-layouts  3.08 us (1%)
    pallas_call x1, Pallas kernels, local(): pl.pallas_call(body, out_shape=jax.ShapeDtypeStruct((W, T), f32), in_spec...  241 us

profile of v1, /device:TPU:101, one launch (start us, length us, event | category | flops | bytes accessed | tf_op | source)
XLA Modules:
  0.0 244.4 jit_solution(10585912896271379930)
XLA Ops:
  0.0 241.3 %two_panels.1 = f32[1024,512]{1,0:T(8,128)} custom-call(f32[1024,512]{1,0:T(8,128)} %a_ref.1), custom_call_target="tpu_custom_call" | custom-call | flops 20000000000 | bytes 8000000 | tf_op jit(solution)/shard_map/two_panels/pallas_call | solution.py:546
  241.3 3.1 %copy.3 = f32[1024,512]{1,0:T(8,128)} copy(f32[1024,512]{1,0:T(8,128)} %two_panels.1) | data formatting | bytes 4194304

commit v2 on v0

v2 whole, which is shorter than its diff:
```python
import functools

import jax
import jax.numpy as jnp
from jax import lax
from jax.experimental import pallas as pl
from jax.experimental.pallas import tpu as pltpu
from jax.sharding import PartitionSpec as P

T = 512
W = 1024
B = 128
H = 256
MESH = pl.DeviceIdType.MESH
NT = (((1,), (1,)), ((), ()))
NN = (((1,), (0,)), ((), ()))


def split(x):
    hi = x.astype(jnp.bfloat16)
    lo = (x - hi.astype(jnp.float32)).astype(jnp.bfloat16)
    return hi, lo


def dot3(a, b, dims=NT):
    (ah, al), (bh, bl) = a, b
    d = functools.partial(
        lax.dot_general, dimension_numbers=dims, preferred_element_type=jnp.float32
    )
    return d(ah, bh) + (d(ah, bl) + d(al, bh))


def lane(x, i):
    return jnp.broadcast_to(x[:, i : i + 1], (8, B))


def sub(x, i):
    return jnp.broadcast_to(x[i : i + 1, :], (8, B))


def chol_block(block):
    n = B // 8
    li = lax.broadcasted_iota(jnp.int32, (8, B), 1)
    si = lax.broadcasted_iota(jnp.int32, (8, B), 0)
    rows = [block[8 * i : 8 * i + 8] for i in range(n)]
    eye = [(li == si + 8 * i).astype(jnp.float32) for i in range(n)]
    upper, inverse = [], []

    def merge(xs):
        out = xs[0]
        for t in range(1, 8):
            out = jnp.where(si == t, xs[t], out)
        return out

    for j in range(n):
        o = 8 * j
        cols = [lane(rows[j], o + q) for q in range(8)]
        m = {(p, q): sub(cols[q], p) for q in range(8) for p in range(q, 8)}
        rb = [sub(rows[j], p) for p in range(8)]
        eb = [sub(eye[j], p) for p in range(8)]
        nxt = j + 1 < n
        if nxt:
            raw = [[lane(rows[i], o + q) for q in range(8)] for i in range(j + 1, n)]
            nc = list(raw[0])
        rk = [None] * 8
        fs = {}
        for k in range(8):
            rk[k] = 1.0 / m[k, k]
            for q in range(k + 1, 8):
                if q == k + 1:
                    m[q, q] = m[q, q] - (m[q, k] * m[q, k]) * rk[k]
                f = m[q, k] * rk[k]
                fs[q, k] = f
                for p in range(q + (1 if q == k + 1 else 0), 8):
                    m[p, q] = m[p, q] - m[p, k] * f
                rb[q] = rb[q] - f * rb[k]
                eb[q] = eb[q] - f * eb[k]
                if nxt:
                    nc[q] = nc[q] - f * nc[k]
            if nxt:
                c = nc[k] * rk[k]
                rows[j + 1] = rows[j + 1] - c * rb[k]
                eye[j + 1] = eye[j + 1] - c * eb[k]
        sk = lax.rsqrt(merge([m[k, k] for k in range(8)]))
        upper.append(merge(rb) * sk)
        inverse.append(merge(eb) * sk)
        if j + 2 < n:
            vr = [rb[k] * rk[k] for k in range(8)]
            ve = [eb[k] * rk[k] for k in range(8)]
            for q in range(7, -1, -1):
                for k in range(q):
                    vr[k] = vr[k] - fs[q, k] * vr[q]
                    ve[k] = ve[k] - fs[q, k] * ve[q]
            for i in range(j + 2, n):
                ar, ae = rows[i], eye[i]
                for q in range(8):
                    c = raw[i - j - 1][q]
                    ar = ar - c * vr[q]
                    ae = ae - c * ve[q]
                rows[i], eye[i] = ar, ae
    return jnp.concatenate(upper, 0), jnp.concatenate(inverse, 0)


def body(
    a_ref, m_ref, rbuf, cbuf, lw, dbuf, work, lref, wref, lh, ll, wh, wl, xh, xl, uh, ul,
    ssem, r1, r2, r3, r4, c0, c1, c2, c3, d1, d2, d3, d5, l4, tsem, lsem,
):
    row = lax.axis_index("row")
    col = lax.axis_index("col")
    h = lax.rem(row, 2)
    z = lax.div(row, 2)
    x = lax.div(col, 4)
    y = lax.rem(col, 4)
    major = jnp.where(h == 0, x, y)
    def put(src, dst, send, recv, row_to, col_to):
        return pltpu.make_async_remote_copy(
            src_ref=src, dst_ref=dst, send_sem=send, recv_sem=recv,
            device_id=(row_to, col_to), device_id_type=MESH,
        )

    def rows(start, size):
        return pl.ds(pl.multiple_of(start * size, size), size)

    barrier = pltpu.get_barrier_semaphore()

    def greet(row_to, col_to):
        pl.semaphore_signal(barrier, inc=1, device_id=(row_to, col_to), device_id_type=MESH)

    @pl.loop(1, 16)
    def _(t):
        greet(row, lax.rem(col + t, 16))
        greet(2 * z + 1 - h, lax.rem(col + t, 16))

    for t in range(1, 4):
        greet(2 * lax.rem(z + t, 4), col)
        greet(2 * lax.rem(z + t, 4) + 1, col)
    greet(2 * z + 1 - h, col)
    load = pltpu.make_async_copy(a_ref, m_ref, lsem.at[0, 2])
    load.start()

    @pl.when(h == 0)
    def _():
        lref[...] = jnp.zeros_like(lref)

    load.wait()
    pl.semaphore_wait(barrier, 37)

    def panel(p):
        first = 2 * p
        second = first + 1
        is_source = (x == 0) & ((y == first) | (y == second))
        root = (row == first) & (col == first)
        half = jnp.where(y == second, 1, 0)
        mycols = pl.ds(pl.multiple_of(half * T, T), T)
        scols = [pl.ds(0, T), pl.ds(T, T)]
        R, C, LW, D = rbuf.at[p], cbuf.at[p], lw.at[p], dbuf.at[p]
        other = 2 * z + 1 - h

        head = D.at[pl.ds(0, B), pl.ds(0, B)]
        parts = ((B, 32, T, 12), (T, 64, W, 8))

        def h_plane(t):
            return put(
                m_ref.at[pl.ds(0, B), pl.ds(0, B)], head, ssem.at[p, 5, t], d5.at[p, 0],
                row, lax.rem(col + t, 16),
            )

        def h_planes(t):
            return put(
                head, head, ssem.at[p, 2, t], d5.at[p, 1], 2 * lax.rem(z + t, 4) + h, col
            )

        def head_start():
            @pl.when(root)
            def _():
                @pl.loop(1, 16)
                def _(t):
                    h_plane(t).start()

                own = pltpu.make_async_copy(
                    m_ref.at[pl.ds(0, B), pl.ds(0, B)], head, lsem.at[p, 2]
                )
                own.start()
                own.wait()
                for t in (1, 2, 3):
                    h_planes(t).start()

        def head_wait():
            @pl.when(z == p)
            def _():
                @pl.when(jnp.logical_not(root))
                def _():
                    h_plane(1).wait_recv()
                    for t in (1, 2, 3):
                        h_planes(t).start()

            @pl.when(z != p)
            def _():
                h_planes(1).wait_recv()

        def d_owner(n):
            return (h == 0) & ((x >= 1) if n == 0 else (lax.rem(x, 2) == 1))

        def d_mine(n):
            return col - 4 if n == 0 else 2 * y + lax.div(x, 2)

        def d_col(n, i):
            return 4 + i if n == 0 else 4 + 8 * lax.rem(i, 2) + lax.div(i, 2)

        def d_piece(n, i):
            start, size, width, _c = parts[n]
            return D.at[pl.ds(pl.multiple_of(start + i * size, size), size), pl.ds(0, width)]

        def d_scatter(n, i, s):
            start, size, width, _c = parts[n]
            here = pl.ds(pl.multiple_of((start if n == 0 else 0) + i * size, size), size)
            there = pl.ds(pl.multiple_of(start + i * size, size), size)
            dst = D.at[there, pl.ds(0, T) if n == 0 else s]
            return put(
                m_ref.at[here, :], dst, ssem.at[p, n, i],
                d1.at[p, n + (half if n else 0)], 2 * z, d_col(n, i),
            )

        def d_source(n):
            return root if n == 0 else is_source & (row == second)

        def d_start(n):
            @pl.when(d_source(n))
            def _():
                @pl.loop(0, parts[n][3])
                def _(i):
                    d_scatter(n, i, mycols).start()

        def d_planes(n, t):
            ref = d_piece(n, d_mine(n))
            return put(
                ref, ref, ssem.at[p, 3 + n, t], d2.at[p, n], 2 * lax.rem(z + t, 4) + h, col
            )

        def d_spread(n, t):
            ref = d_piece(n, d_mine(n))
            return put(
                ref, ref, ssem.at[p, 6 + n, t], d3.at[p, n, d_mine(n)],
                row, lax.rem(col + t, 16),
            )

        def d_forward(n):
            @pl.when(d_owner(n))
            def _():
                @pl.when(z == p)
                def _():
                    for s in range(1 + n):
                        ref = D.at[
                            pl.ds(
                                pl.multiple_of(
                                    parts[n][0] + d_mine(n) * parts[n][1], 32
                                ),
                                parts[n][1],
                            ),
                            scols[s],
                        ]
                        put(ref, ref, ssem.at[p, n, 0], d1.at[p, n + s], row, col).wait_recv()
                    for t in (1, 2, 3):
                        d_planes(n, t).start()

                @pl.when(z != p)
                def _():
                    d_planes(n, 1).wait_recv()

                if n == 0:
                    @pl.loop(1, 16)
                    def _(t):
                        d_spread(n, t).start()
                else:
                    for t in (1, 3, 2):
                        e_row(t).start()

        def e_row(t):
            ref = d_piece(1, d_mine(1))
            return put(
                ref, ref, ssem.at[p, 7, t], d3.at[p, 1, lax.div(x, 2)],
                row, 4 * lax.rem(x + t, 4) + y,
            )

        def e_rows(of):
            return D.at[pl.ds(pl.multiple_of(T + of * 128, 128), 128), :]

        def e_column(t):
            ref = e_rows(y)
            return put(
                ref, ref, ssem.at[p, 7, 4 + t], d3.at[p, 1, 1 + t],
                row, 4 * x + lax.rem(y + t, 4),
            )

        def e_across():
            for i in range(2):
                @pl.when(x != 1 + 2 * i)
                def _():
                    ref = d_piece(1, 2 * y + i)
                    put(ref, ref, ssem.at[p, 7, 0], d3.at[p, 1, i], row, col).wait_recv()

            for t in (1, 3, 2):
                e_column(t).start()

        def e_gather():
            for t in (1, 3, 2):
                ref = e_rows(lax.rem(y + 4 - t, 4))
                put(ref, ref, ssem.at[p, 7, 0], d3.at[p, 1, 1 + t], row, col).wait_recv()

        def d_gather(n):
            @pl.loop(0, parts[n][3])
            def _(i):
                @pl.when(col != d_col(n, i))
                def _():
                    ref = d_piece(n, i)
                    put(
                        ref, ref, ssem.at[p, 6 + n, 0], d3.at[p, n, i], row, col
                    ).wait_recv()

        last_tile = lref.at[pl.ds(T, T), pl.ds(T, T)]

        def last_send():
            return put(last_tile, last_tile, ssem.at[p, 8, 5], tsem.at[p], other, col)

        def r_place(q):
            return (x, y) if q == 0 else (y, x)

        def r_col(q, ma, mi):
            return 4 * ma + mi if q == 0 else 4 * mi + ma

        def r_scatter(i):
            to = jnp.where(h == 0, i, 4 * lax.rem(i, 4) + lax.div(i, 4))
            return put(
                m_ref.at[rows(i, 64), :], R.at[h, rows(i, 64), mycols],
                ssem.at[p, 13, i], r1.at[p, h, half], 2 * z + 1, to,
            )

        def r_own(fn):
            @pl.loop(0, 16)
            def _(i):
                @pl.when((h == 0) | (i != 4 * y + x))
                def _():
                    fn(i)

        def r_piece(q, ma, mi):
            return R.at[q, rows(4 * ma + mi, 64), :]

        def r_minor(q, t):
            ma, mi = r_place(q)
            ref = r_piece(q, ma, mi)
            return put(
                ref, ref, ssem.at[p, 16 + q, t - 1], r2.at[p, q, t - 1],
                row, r_col(q, ma, lax.rem(mi + t, 4)),
            )

        def r_minor_in(q, t):
            ma, mi = r_place(q)
            ref = r_piece(q, ma, lax.rem(mi + 4 - t, 4))
            put(ref, ref, ssem.at[p, 16, 0], r2.at[p, q, t - 1], row, col).wait_recv()

        def r_major(q, slot, t):
            ma, mi = r_place(q)
            ref = r_piece(q, ma, lax.rem(mi + 4 - slot, 4))
            return put(
                ref, ref, ssem.at[p, 16 + q, 3 + 3 * slot + t - 1], r3.at[p, q, 3 * slot + t - 1],
                row, r_col(q, lax.rem(ma + t, 4), mi),
            )

        def r_major_in(q, t):
            ma, mi = r_place(q)
            for slot in range(4):
                ref = r_piece(q, lax.rem(ma + 4 - t, 4), lax.rem(mi + 4 - slot, 4))
                put(
                    ref, ref, ssem.at[p, 16, 0], r3.at[p, q, 3 * slot + t - 1], row, col
                ).wait_recv()

        def r_core(t):
            ref = R.at[0, rows(lax.rem(x + 4 - t, 4), 256), :]
            return put(ref, ref, ssem.at[p, 18, t], r4.at[p, t], 2 * z, col)

        def r_first():
            for q in range(2):
                for s in range(2):
                    there = put(
                        m_ref.at[rows(0, 64), :], R.at[q, rows(0, 64), scols[s]],
                        ssem.at[p, 13, 0], r1.at[p, q, s], row, col,
                    )
                    if q == 0:
                        there.wait_recv()
                    else:
                        pl.when(jnp.logical_not((x == 0) & (y == first + s)))(there.wait_recv)
                for t in (1, 3, 2):
                    r_minor(q, t).start()
                for t in (1, 3, 2):
                    r_major(q, 0, t).start()

        def r_second():
            for slot in (1, 3, 2):
                for q in range(2):
                    r_minor_in(q, slot)
                    for t in (1, 3, 2):
                        r_major(q, slot, t).start()

        def c_rows(hh, q):
            return pl.ds(pl.multiple_of(hh * T + q * B, B), B)

        def c_tile(hh):
            return C.at[pl.ds(pl.multiple_of(hh * T, T), T), :]

        def c_first(t, which):
            zt = lax.rem(z + t, 4)
            q = zt if which == 0 else z
            return put(
                m_ref.at[rows(q, B), :], C.at[c_rows(h, q), :],
                ssem.at[p, 15, 2 * (t - 1) + which], c1.at[p, h, which], 2 * zt + 1, col,
            )

        def c_first_in(hh, which):
            ref = C.at[c_rows(hh, z if which == 0 else p), :]
            put(ref, ref, ssem.at[p, 15, 0], c1.at[p, hh, which], row, col).wait_recv()

        def c_second(hh, t):
            ref = C.at[c_rows(hh, z), :]
            return put(
                ref, ref, ssem.at[p, 14, 3 * hh + t - 1], c2.at[p, hh, t - 1],
                2 * lax.rem(z + t, 4) + 1, col,
            )

        def c_second_in(hh, t):
            ref = C.at[c_rows(hh, lax.rem(z + 4 - t, 4)), :]
            put(ref, ref, ssem.at[p, 14, 0], c2.at[p, hh, t - 1], row, col).wait_recv()

        def c_sibling():
            return put(
                m_ref.at[pl.ds(0, T), :], c_tile(0), ssem.at[p, 8, 7], c0.at[p], other, col
            )

        def c_core():
            return put(C, C, ssem.at[p, 8, 6], c3.at[p], other, col)

        def c_start():
            @pl.when(z == p)
            def _():
                for t in (1, 3, 2):
                    for which in (0, 1):
                        c_first(t, which).start()

                @pl.when(h == 0)
                def _():
                    c_sibling().start()

                @pl.when(h == 1)
                def _():
                    own = pltpu.make_async_copy(
                        m_ref.at[pl.ds(0, T), :], c_tile(1), lsem.at[p, 1]
                    )
                    own.start()
                    own.wait()

        def c_forward():
            @pl.when(z != p)
            def _():
                for hh in range(2):
                    c_first_in(hh, 0)
                    for t in (1, 2, 3):
                        @pl.when(lax.rem(z + t, 4) != p)
                        def _():
                            c_second(hh, t).start()

        def c_cross():
            @pl.when(z != p)
            def _():
                for hh in range(2):
                    c_first_in(hh, 1)
                    for t in (1, 2, 3):
                        @pl.when(lax.rem(z + 4 - t, 4) != p)
                        def _():
                            c_second_in(hh, t)

            @pl.when(z == p)
            def _():
                c_sibling().wait_recv()

        def l_core(g):
            ref = LW.at[pl.ds(g * H, W - g * H), pl.ds(g * H, H)]
            return put(ref, ref, ssem.at[p, 8, 1 + g], l4.at[p, g], other, col)

        d_start(0)
        head_start()
        d_start(1)

        @pl.when(is_source)
        def _():
            r_own(lambda i: r_scatter(i).start())

            @pl.when(h == 1)
            def _():
                own = pltpu.make_async_copy(
                    m_ref.at[rows(4 * y + x, 64), :],
                    R.at[1, rows(4 * y + x, 64), mycols], lsem.at[p, 0],
                )
                own.start()
                own.wait()

        def close(g, w0, l10, w1):
            low = dot3(split(w1), split(dot3(split(l10), split(w0), NN)), NN)
            big = jnp.concatenate(
                [
                    jnp.concatenate([w0, jnp.zeros_like(w0)], 1),
                    jnp.concatenate([-low, w1], 1),
                ],
                0,
            )
            wh[g], wl[g] = split(big)
            return big

        right_of = col > second
        in_panel = (col == first) | (col == second)
        top_below = row > second
        top_band = (row == first) | (row == second)
        column_half = jnp.where(col == second, 1, 0)

        def absorb(g):
            ds = pl.ds(g * H, H)
            wh[g], wl[g] = split(LW[ds, ds])
            for j in range(g + 1, 4):
                js = pl.ds(j * H, H)
                lh[js, ds], ll[js, ds] = split(LW[js, ds])

        def block(i):
            return pl.ds(i * H, H)

        def u_value(kb, cs):
            ks, done = block(kb), pl.ds(0, kb * H)
            value = C[ks, cs]
            if kb:
                value = value - dot3(
                    (lh[ks, done], ll[ks, done]), (uh[done, cs], ul[done, cs]), NN
                )
            return value

        def u_step(kb, ready=False):
            for n in range(2):
                cs = block(n)
                value = C[block(kb), cs] if ready else u_value(kb, cs)
                uk = dot3((wh[kb], wl[kb]), split(value), NN)
                uh[block(kb), cs], ul[block(kb), cs] = split(uk)
                if not ready:
                    C[block(kb), cs] = uk

        def u_ahead():
            for n in range(2):
                C[block(3), block(n)] = u_value(3, block(n))

        def x_value(q, g, kb):
            rs, ks, done = rows(g, H), block(kb), pl.ds(0, kb * H)
            value = R[q, rs, ks]
            if kb:
                value = value - dot3(
                    (xh[rs, done], xl[rs, done]), (lh[ks, done], ll[ks, done])
                )
            return value

        def keep_x(g, kb, xk):
            @pl.when(((g >= 2) | top_below) & in_panel & (column_half == kb // 2))
            def _():
                m_ref[rows(g, H), pl.ds(kb % 2 * H, H)] = xk

        def x_group(q, g):
            rs = rows(g, H)
            for kb in range(3):
                xk = dot3(split(x_value(q, g, kb)), (wh[kb], wl[kb]))
                xh[rs, block(kb)], xl[rs, block(kb)] = split(xk)
                if q:
                    keep_x(g, kb, xk)
                else:
                    R[q, rs, block(kb)] = xk
            R[q, rs, block(3)] = x_value(q, g, 3)

        def x_last(g):
            rs = rows(g, H)
            xk = dot3(split(R[h, rs, block(3)]), (wh[3], wl[3]))
            xh[rs, block(3)], xl[rs, block(3)] = split(xk)
            keep_x(g, 3, xk)

        def update(g):
            @pl.when(((g >= 2) | top_below) & right_of)
            def _():
                rs = rows(g, H)
                for n in range(2):
                    cs = pl.ds(n * H, H)
                    m_ref[rs, cs] = m_ref[rs, cs] - dot3(
                        (xh[rs, :], xl[rs, :]), (uh[:, cs], ul[:, cs]), NN
                    )

        def both(kb):
            u_step(kb)
            x_step(major, kb)

        def drain_source():
            for n in range(2):
                @pl.when(d_source(n))
                def _():
                    @pl.loop(0, parts[n][3])
                    def _(i):
                        d_scatter(n, i, mycols).wait_send()

            @pl.when(root)
            def _():
                @pl.loop(1, 16)
                def _(t):
                    h_plane(t).wait_send()

            @pl.when(is_source)
            def _():
                r_own(lambda i: r_scatter(i).wait_send())

            @pl.when(z == p)
            def _():
                for t in (1, 2, 3):
                    for which in (0, 1):
                        c_first(t, which).wait_send()

                @pl.when(h == 0)
                def _():
                    c_sibling().wait_send()

        def drain_r():
            for q in range(2):
                for t in (1, 2, 3):
                    r_minor(q, t).wait_send()
                    for slot in range(4):
                        r_major(q, slot, t).wait_send()

        def drain_c():
            @pl.when(z != p)
            def _():
                for t in (1, 2, 3):
                    @pl.when(lax.rem(z + t, 4) != p)
                    def _():
                        for hh in range(2):
                            c_second(hh, t).wait_send()

        @pl.when(h == 0)
        def _():
            head_wait()
            d_forward(0)
            d_forward(1)
            c_start()
            work[0:B, 0:B] = D[0:B, 0:B]

            def keep(rs, cs, value):
                lref[rs, cs] = value
                LW[rs, cs] = value
                pair_ = split(value)
                lh[rs, cs], ll[rs, cs] = pair_
                return pair_

            def close_root(g):
                s0, s1 = slice(g * H, g * H + B), slice(g * H + B, g * H + H)
                big = close(g, wref[s0, :], lref[s1, s0], wref[s1, :])
                LW[g * H : g * H + H, g * H : g * H + H] = big
                return wh[g], wl[g]

            def send(g):
                l_core(g).start()

            @pl.loop(0, W // B)
            def _(k):
                q0, q1, q2, q3 = (slice(i * H, i * H + H) for i in range(4))

                @pl.when(k == 1)
                def _():
                    e_across()
                    d_gather(0)
                    work[B:H, 0:H] = D[B:H, 0:H]

                @pl.when(k == 2)
                def _():
                    w = close_root(0)
                    xs = keep(q1, q0, dot3(split(D[q1, q0]), w))
                    work[q1, q1] = D[q1, q1] - dot3(xs, xs)

                @pl.when(k == 4)
                def _():
                    w = close_root(1)
                    e_gather()
                    es = keep(slice(T, W), q0, dot3(split(D[T:W, q0]), (wh[0], wl[0])))
                    send(0)
                    rest = D[T:W, q1] - dot3(es, (lh[q1, q0], ll[q1, q0]))
                    keep(slice(T, W), q1, dot3(split(rest), w))
                    send(1)
                    left = lambda r: (lh[r, 0:T], ll[r, 0:T])
                    work[q2, q2] = D[q2, q2] - dot3(left(q2), left(q2))
                    work[q3, q2] = D[q3, q2] - dot3(left(q3), left(q2))
                    work[q3, q3] = D[q3, q3] - dot3(left(q3), left(q3))

                @pl.when(k == 6)
                def _():
                    w = close_root(2)
                    xs = keep(q3, q2, dot3(split(work[q3, q2]), w))
                    send(2)
                    work[q3, q3] = work[q3, q3] - dot3(xs, xs)

                o = pl.multiple_of(k * B, B)
                here = pl.ds(o, B)
                before = pl.ds(pl.multiple_of(jnp.maximum(o - B, 0), B), B)

                @pl.when(lax.rem(k, 2) == 1)
                def _():
                    xk = dot3(split(work[here, before]), split(wref[before, :]))
                    lref[here, before] = xk
                    xs = split(xk)
                    work[here, here] = work[here, here] - dot3(xs, xs)

                upper, inverse = chol_block(work[here, here])
                wref[here, :] = inverse
                ri = lax.broadcasted_iota(jnp.int32, (B, B), 0)
                ci = lax.broadcasted_iota(jnp.int32, (B, B), 1)
                lref[here, here] = jnp.where(ri >= ci, upper.T, 0.0)

            close_root(3)
            l_core(3).start()

            @pl.when((row == first) & (col == second))
            def _():
                last_send().start()

            drain_source()
            c_core().wait_recv()
            for kb in range(3):
                uh[block(kb), :], ul[block(kb), :] = split(C[block(kb), :])
            for t in range(4):
                r_core(t).wait_recv()

            @pl.loop(0, 4)
            def _(g):
                rs = rows(g, H)
                for kb in range(3):
                    xk = R[0, rs, block(kb)]
                    xh[rs, block(kb)], xl[rs, block(kb)] = split(xk)
                    keep_x(g, kb, xk)

        @pl.when(h == 1)
        def _():
            r_first()
            c_start()
            c_forward()
            r_second()
            c_cross()
            drain_source()
            drain_c()
            for kb in range(3):
                l_core(kb).wait_recv()
                absorb(kb)
                u_step(kb)
            u_ahead()
            c_core().start()
            for q in range(2):
                for t in (1, 3, 2):
                    r_major_in(q, t)
            drain_r()

            @pl.loop(0, 4)
            def _(t):
                g = lax.rem(x + 4 - t, 4)
                x_group(0, g)
                r_core(t).start()

            @pl.loop(0, 4)
            def _(g):
                x_group(1, g)

            l_core(3).wait_recv()
            absorb(3)

        u_step(3, True)

        @pl.loop(0, 4)
        def _(g):
            x_last(g)
            update(g)

        @pl.when(top_band & right_of)
        def _():
            m_ref[0:T, :] = jnp.zeros((T, T), jnp.float32)

        @pl.when(top_band & in_panel)
        def _():
            @pl.when(root)
            def _():
                m_ref[0:T, :] = lref[0:T, 0:T]

            @pl.when((row == first) & (col == second))
            def _():
                m_ref[0:T, :] = jnp.zeros((T, T), jnp.float32)

            @pl.when((row == second) & (col == first))
            def _():
                m_ref[0:T, :] = LW[T:W, 0:T]

            @pl.when((row == second) & (col == second))
            def _():
                last_send().wait_recv()
                m_ref[0:T, :] = last_tile[...]

        @pl.when(h == 1)
        def _():
            for t in range(4):
                r_core(t).wait_send()

        @pl.when(h == 1)
        def _():
            c_core().wait_send()

        for n in range(2):
            @pl.when(d_owner(n))
            def _():
                @pl.when(z == p)
                def _():
                    for t in (1, 2, 3):
                        d_planes(n, t).wait_send()

                if n == 0:
                    @pl.loop(1, 16)
                    def _(t):
                        d_spread(n, t).wait_send()
                else:
                    for t in (1, 3, 2):
                        e_row(t).wait_send()

        @pl.when(h == 0)
        def _():
            for t in (1, 3, 2):
                e_column(t).wait_send()
            for g in range(4):
                l_core(g).wait_send()

            @pl.when(z == p)
            def _():
                for t in (1, 2, 3):
                    h_planes(t).wait_send()

            @pl.when((row == first) & (col == second))
            def _():
                last_send().wait_send()

    pl.loop(0, 2)(panel)


def local(kernel):
    f32, b16 = jnp.float32, jnp.bfloat16
    dma = pltpu.SemaphoreType.DMA
    return pl.pallas_call(
        body,
        out_shape=jax.ShapeDtypeStruct((W, T), f32),
        in_specs=[pl.BlockSpec(memory_space=pl.ANY)],
        out_specs=pl.BlockSpec(memory_space=pltpu.VMEM),
        scratch_shapes=[
            pltpu.VMEM((2, 2, W, W), f32),
            pltpu.VMEM((2, W, T), f32),
            pltpu.VMEM((2, W, W), f32),
            pltpu.VMEM((2, W, W), f32),
            pltpu.VMEM((W, W), f32),
            pltpu.VMEM((W, W), f32),
            pltpu.VMEM((W, B), f32),
            pltpu.VMEM((W, W), b16),
            pltpu.VMEM((W, W), b16),
            pltpu.VMEM((4, H, H), b16),
            pltpu.VMEM((4, H, H), b16),
            pltpu.VMEM((W, W), b16),
            pltpu.VMEM((W, W), b16),
            pltpu.VMEM((W, T), b16),
            pltpu.VMEM((W, T), b16),
            dma((2, 19, 16)),
            dma((2, 2, 2)), dma((2, 2, 3)), dma((2, 2, 12)), dma((2, 4)),
            dma((2,)), dma((2, 2, 2)), dma((2, 2, 3)), dma((2,)),
            dma((2, 3)), dma((2, 2)), dma((2, 2, 12)), dma((2, 2)),
            dma((2, 4)),
            dma((2,)),
            dma((2, 3)),
        ],
        compiler_params=pltpu.CompilerParams(
            collective_id=0, has_side_effects=True, vmem_limit_bytes=62 * 1024 * 1024
        ),
        cost_estimate=pl.CostEstimate(
            flops=20_000_000_000, bytes_accessed=8_000_000, transcendentals=0
        ),
        name="two_panels",
    )(kernel)


def solution(mesh):
    return jax.shard_map(
        local,
        mesh=mesh,
        in_specs=(P("row", "col"),),
        out_specs=P("row", "col"),
        check_vma=False,
    )
```

time: 1350 us -> 215 us (0.16)
  the two profiles are of different devices: /device:TPU:101 before, /device:TPU:119 now
where the time goes in v2:
time: 215 us
  Pallas kernels  212 us (99%)
  local copies, waits for them, and re-layouts  3.08 us (1%)
    pallas_call x1, Pallas kernels, local(): pl.pallas_call(body, out_shape=jax.ShapeDtypeStruct((W, T), f32), in_spec...  212 us

profile of v2, /device:TPU:119, one launch (start us, length us, event | category | flops | bytes accessed | tf_op | source)
XLA Modules:
  0.0 214.7 jit_solution(15020503393543763568)
XLA Ops:
  0.0 211.6 %two_panels.1 = f32[1024,512]{1,0:T(8,128)} custom-call(f32[1024,512]{1,0:T(8,128)} %a_ref.1), custom_call_target="tpu_custom_call" | custom-call | flops 20000000000 | bytes 8000000 | tf_op jit(solution)/shard_map/two_panels/pallas_call | solution.py:854
  211.6 3.1 %copy.3 = f32[1024,512]{1,0:T(8,128)} copy(f32[1024,512]{1,0:T(8,128)} %two_panels.1) | data formatting | bytes 4194304

commit v3 on v2

--- a/solution.py
+++ b/solution.py
@@ -135,6 +135,15 @@
         greet(2 * lax.rem(z + t, 4), col)
         greet(2 * lax.rem(z + t, 4) + 1, col)
     greet(2 * z + 1 - h, col)
+
+    @pl.when((h == 0) & (x == 0))
+    def _():
+        @pl.loop(0, 32)
+        def _(i):
+            @pl.when((lax.div(i, 4) != row) | (lax.rem(i, 4) != col))
+            def _():
+                greet(lax.div(i, 4), lax.rem(i, 4))
+
     load = pltpu.make_async_copy(a_ref, m_ref, lsem.at[0, 2])
     load.start()
 
@@ -143,7 +152,17 @@
         lref[...] = jnp.zeros_like(lref)
 
     load.wait()
-    pl.semaphore_wait(barrier, 37)
+    @pl.when(x != 0)
+    def _():
+        pl.semaphore_wait(barrier, 37)
+
+    @pl.when((x == 0) & (h == 0))
+    def _():
+        pl.semaphore_wait(barrier, 52)
+
+    @pl.when((x == 0) & (h == 1))
+    def _():
+        pl.semaphore_wait(barrier, 53)
 
     def panel(p):
         first = 2 * p
@@ -157,7 +176,7 @@
         other = 2 * z + 1 - h
 
         head = D.at[pl.ds(0, B), pl.ds(0, B)]
-        parts = ((B, 32, T, 12), (T, 64, W, 8))
+        parts = ((B, 24, T), (T, 32, W))
 
         def h_plane(t):
             return put(
@@ -198,124 +217,94 @@
             def _():
                 h_planes(1).wait_recv()
 
-        def d_owner(n):
-            return (h == 0) & ((x >= 1) if n == 0 else (lax.rem(x, 2) == 1))
-
-        def d_mine(n):
-            return col - 4 if n == 0 else 2 * y + lax.div(x, 2)
-
-        def d_col(n, i):
-            return 4 + i if n == 0 else 4 + 8 * lax.rem(i, 2) + lax.div(i, 2)
-
-        def d_piece(n, i):
-            start, size, width, _c = parts[n]
-            return D.at[pl.ds(pl.multiple_of(start + i * size, size), size), pl.ds(0, width)]
+        def d_rows(n, i, count=1):
+            start, size, width = parts[n]
+            return D.at[
+                pl.ds(pl.multiple_of(start + i * size, 8), count * size), pl.ds(0, width)
+            ]
 
         def d_scatter(n, i, s):
-            start, size, width, _c = parts[n]
-            here = pl.ds(pl.multiple_of((start if n == 0 else 0) + i * size, size), size)
-            there = pl.ds(pl.multiple_of(start + i * size, size), size)
-            dst = D.at[there, pl.ds(0, T) if n == 0 else s]
-            return put(
-                m_ref.at[here, :], dst, ssem.at[p, n, i],
-                d1.at[p, n + (half if n else 0)], 2 * z, d_col(n, i),
+            start, size, _w = parts[n]
+            here = pl.ds(pl.multiple_of((0 if n else start) + i * size, 8), size)
+            there = pl.ds(pl.multiple_of(start + i * size, 8), size)
+            return (
+                m_ref.at[here, :], D.at[there, s if n else pl.ds(0, T)],
+                ssem.at[p, n, i], d1.at[p, n + (half if n else 0)],
+                2 * lax.div(i, 4), lax.rem(i, 4),
             )
 
         def d_source(n):
-            return root if n == 0 else is_source & (row == second)
+            return is_source & (row == second) if n else root
+
+        def d_out(n, fn):
+            @pl.loop(0, 16)
+            def _(i):
+                if n:
+                    fn(put(*d_scatter(n, i, mycols)))
+                else:
+                    @pl.when(i != d_mine)
+                    def _():
+                        fn(put(*d_scatter(n, i, mycols)))
+
+        d_mine = 4 * z + y
 
         def d_start(n):
             @pl.when(d_source(n))
             def _():
-                @pl.loop(0, parts[n][3])
-                def _(i):
-                    d_scatter(n, i, mycols).start()
-
-        def d_planes(n, t):
-            ref = d_piece(n, d_mine(n))
-            return put(
-                ref, ref, ssem.at[p, 3 + n, t], d2.at[p, n], 2 * lax.rem(z + t, 4) + h, col
-            )
-
-        def d_spread(n, t):
-            ref = d_piece(n, d_mine(n))
-            return put(
-                ref, ref, ssem.at[p, 6 + n, t], d3.at[p, n, d_mine(n)],
-                row, lax.rem(col + t, 16),
+                d_out(n, lambda c: c.start())
+                if n == 0:
+                    src, dst = d_scatter(n, d_mine, mycols)[:2]
+                    own = pltpu.make_async_copy(src, dst, lsem.at[p, 3])
+                    own.start()
+                    own.wait()
+
+        def d_x(n, t):
+            ref = d_rows(n, d_mine)
+            return put(
+                ref, ref, ssem.at[p, 3 + n, t], d2.at[p, n], row, 4 * lax.rem(x + t, 4) + y
+            )
+
+        def d_y(n, t):
+            ref = d_rows(n, d_mine)
+            return put(
+                ref, ref, ssem.at[p, 6 + n, t], d3.at[p, n, t], row, 4 * x + lax.rem(y + t, 4)
+            )
+
+        def d_z(n, t):
+            ref = d_rows(n, 4 * z, 4)
+            return put(
+                ref, ref, ssem.at[p, 6 + n, 4 + t], d3.at[p, n, 4 + t],
+                2 * lax.rem(z + t, 4) + h, col,
             )
 
         def d_forward(n):
-            @pl.when(d_owner(n))
-            def _():
-                @pl.when(z == p)
-                def _():
-                    for s in range(1 + n):
-                        ref = D.at[
-                            pl.ds(
-                                pl.multiple_of(
-                                    parts[n][0] + d_mine(n) * parts[n][1], 32
-                                ),
-                                parts[n][1],
-                            ),
-                            scols[s],
-                        ]
-                        put(ref, ref, ssem.at[p, n, 0], d1.at[p, n + s], row, col).wait_recv()
-                    for t in (1, 2, 3):
-                        d_planes(n, t).start()
-
-                @pl.when(z != p)
-                def _():
-                    d_planes(n, 1).wait_recv()
-
-                if n == 0:
-                    @pl.loop(1, 16)
-                    def _(t):
-                        d_spread(n, t).start()
-                else:
-                    for t in (1, 3, 2):
-                        e_row(t).start()
-
-        def e_row(t):
-            ref = d_piece(1, d_mine(1))
-            return put(
-                ref, ref, ssem.at[p, 7, t], d3.at[p, 1, lax.div(x, 2)],
-                row, 4 * lax.rem(x + t, 4) + y,
-            )
-
-        def e_rows(of):
-            return D.at[pl.ds(pl.multiple_of(T + of * 128, 128), 128), :]
-
-        def e_column(t):
-            ref = e_rows(y)
-            return put(
-                ref, ref, ssem.at[p, 7, 4 + t], d3.at[p, 1, 1 + t],
-                row, 4 * x + lax.rem(y + t, 4),
-            )
-
-        def e_across():
-            for i in range(2):
-                @pl.when(x != 1 + 2 * i)
-                def _():
-                    ref = d_piece(1, 2 * y + i)
-                    put(ref, ref, ssem.at[p, 7, 0], d3.at[p, 1, i], row, col).wait_recv()
-
+            @pl.when(x == 0)
+            def _():
+                for s in range(1 + n):
+                    here = put(*d_scatter(n, d_mine, scols[s])[:3], d1.at[p, n + s], row, col)
+                    if n:
+                        here.wait_recv()
+                    else:
+                        pl.when(jnp.logical_not(root))(here.wait_recv)
+                for t in (1, 3, 2):
+                    d_x(n, t).start()
+
+        def d_second(n):
+            pl.when(x != 0)(d_x(n, 1).wait_recv)
             for t in (1, 3, 2):
-                e_column(t).start()
-
-        def e_gather():
+                d_y(n, t).start()
+
+        def d_third(n):
             for t in (1, 3, 2):
-                ref = e_rows(lax.rem(y + 4 - t, 4))
-                put(ref, ref, ssem.at[p, 7, 0], d3.at[p, 1, 1 + t], row, col).wait_recv()
+                ref = d_rows(n, 4 * z + lax.rem(y + 4 - t, 4))
+                put(ref, ref, ssem.at[p, 6 + n, 0], d3.at[p, n, t], row, col).wait_recv()
+            for t in (1, 3, 2):
+                d_z(n, t).start()
 
         def d_gather(n):
-            @pl.loop(0, parts[n][3])
-            def _(i):
-                @pl.when(col != d_col(n, i))
-                def _():
-                    ref = d_piece(n, i)
-                    put(
-                        ref, ref, ssem.at[p, 6 + n, 0], d3.at[p, n, i], row, col
-                    ).wait_recv()
+            for t in (1, 3, 2):
+                ref = d_rows(n, 4 * lax.rem(z + 4 - t, 4), 4)
+                put(ref, ref, ssem.at[p, 6 + n, 0], d3.at[p, n, 4 + t], row, col).wait_recv()
 
         last_tile = lref.at[pl.ds(T, T), pl.ds(T, T)]
 
@@ -407,12 +396,12 @@
         def c_tile(hh):
             return C.at[pl.ds(pl.multiple_of(hh * T, T), T), :]
 
-        def c_first(t, which):
+        def c_first(hh, t, which):
             zt = lax.rem(z + t, 4)
-            q = zt if which == 0 else z
-            return put(
-                m_ref.at[rows(q, B), :], C.at[c_rows(h, q), :],
-                ssem.at[p, 15, 2 * (t - 1) + which], c1.at[p, h, which], 2 * zt + 1, col,
+            ref = C.at[c_rows(hh, zt if which == 0 else z), :]
+            return put(
+                ref, ref, ssem.at[p, 15, 6 * hh + 2 * (t - 1) + which], c1.at[p, hh, which],
+                2 * zt + 1, col,
             )
 
         def c_first_in(hh, which):
@@ -439,23 +428,19 @@
             return put(C, C, ssem.at[p, 8, 6], c3.at[p], other, col)
 
         def c_start():
-            @pl.when(z == p)
-            def _():
-                for t in (1, 3, 2):
-                    for which in (0, 1):
-                        c_first(t, which).start()
-
-                @pl.when(h == 0)
-                def _():
-                    c_sibling().start()
-
-                @pl.when(h == 1)
-                def _():
-                    own = pltpu.make_async_copy(
-                        m_ref.at[pl.ds(0, T), :], c_tile(1), lsem.at[p, 1]
-                    )
-                    own.start()
-                    own.wait()
+            @pl.when((z == p) & (h == 1))
+            def _():
+                own = pltpu.make_async_copy(
+                    m_ref.at[pl.ds(0, T), :], c_tile(1), lsem.at[p, 1]
+                )
+                own.start()
+                own.wait()
+                for hh in (1, 0):
+                    if hh == 0:
+                        c_sibling().wait_recv()
+                    for t in (1, 3, 2):
+                        for which in (0, 1):
+                            c_first(hh, t, which).start()
 
         def c_forward():
             @pl.when(z != p)
@@ -477,10 +462,6 @@
                         def _():
                             c_second_in(hh, t)
 
-            @pl.when(z == p)
-            def _():
-                c_sibling().wait_recv()
-
         def l_core(g):
             ref = LW.at[pl.ds(g * H, W - g * H), pl.ds(g * H, H)]
             return put(ref, ref, ssem.at[p, 8, 1 + g], l4.at[p, g], other, col)
@@ -488,6 +469,10 @@
         d_start(0)
         head_start()
         d_start(1)
+
+        @pl.when((z == p) & (h == 0))
+        def _():
+            c_sibling().start()
 
         @pl.when(is_source)
         def _():
@@ -601,9 +586,7 @@
             for n in range(2):
                 @pl.when(d_source(n))
                 def _():
-                    @pl.loop(0, parts[n][3])
-                    def _(i):
-                        d_scatter(n, i, mycols).wait_send()
+                    d_out(n, lambda c: c.wait_send())
 
             @pl.when(root)
             def _():
@@ -615,15 +598,16 @@
             def _():
                 r_own(lambda i: r_scatter(i).wait_send())
 
-            @pl.when(z == p)
-            def _():
-                for t in (1, 2, 3):
-                    for which in (0, 1):
-                        c_first(t, which).wait_send()
-
-                @pl.when(h == 0)
-                def _():
-                    c_sibling().wait_send()
+            @pl.when((z == p) & (h == 1))
+            def _():
+                for hh in range(2):
+                    for t in (1, 2, 3):
+                        for which in (0, 1):
+                            c_first(hh, t, which).wait_send()
+
+            @pl.when((z == p) & (h == 0))
+            def _():
+                c_sibling().wait_send()
 
         def drain_r():
             for q in range(2):
@@ -646,7 +630,9 @@
             head_wait()
             d_forward(0)
             d_forward(1)
-            c_start()
+            d_second(0)
+            d_third(0)
+            d_second(1)
             work[0:B, 0:B] = D[0:B, 0:B]
 
             def keep(rs, cs, value):
@@ -671,7 +657,7 @@
 
                 @pl.when(k == 1)
                 def _():
-                    e_across()
+                    d_third(1)
                     d_gather(0)
                     work[B:H, 0:H] = D[B:H, 0:H]
 
@@ -684,7 +670,7 @@
                 @pl.when(k == 4)
                 def _():
                     w = close_root(1)
-                    e_gather()
+                    d_gather(1)
                     es = keep(slice(T, W), q0, dot3(split(D[T:W, q0]), (wh[0], wl[0])))
                     send(0)
                     rest = D[T:W, q1] - dot3(es, (lh[q1, q0], ll[q1, q0]))
@@ -743,8 +729,8 @@
 
         @pl.when(h == 1)
         def _():
+            c_start()
             r_first()
-            c_start()
             c_forward()
             r_second()
             c_cross()
@@ -813,26 +799,18 @@
         def _():
             c_core().wait_send()
 
-        for n in range(2):
-            @pl.when(d_owner(n))
-            def _():
-                @pl.when(z == p)
-                def _():
-                    for t in (1, 2, 3):
-                        d_planes(n, t).wait_send()
-
-                if n == 0:
-                    @pl.loop(1, 16)
-                    def _(t):
-                        d_spread(n, t).wait_send()
-                else:
-                    for t in (1, 3, 2):
-                        e_row(t).wait_send()
-
         @pl.when(h == 0)
         def _():
-            for t in (1, 3, 2):
-                e_column(t).wait_send()
+            for n in range(2):
+                for t in (1, 3, 2):
+                    d_y(n, t).wait_send()
+                    d_z(n, t).wait_send()
+
+                @pl.when(x == 0)
+                def _():
+                    for t in (1, 3, 2):
+                        d_x(n, t).wait_send()
+
             for g in range(4):
                 l_core(g).wait_send()
 
@@ -878,7 +856,7 @@
             dma((2, 3)), dma((2, 2)), dma((2, 2, 12)), dma((2, 2)),
             dma((2, 4)),
             dma((2,)),
-            dma((2, 3)),
+            dma((2, 4)),
         ],
         compiler_params=pltpu.CompilerParams(
             collective_id=0, has_side_effects=True, vmem_limit_bytes=62 * 1024 * 1024

time: 215 us -> 201 us (0.935)
  the two profiles are of different devices: /device:TPU:119 before, /device:TPU:101 now
where the time goes in v3:
time: 201 us
  Pallas kernels  198 us (99%)
  local copies, waits for them, and re-layouts  3.08 us (2%)
    pallas_call x1, Pallas kernels, local(): pl.pallas_call(body, out_shape=jax.ShapeDtypeStruct((W, T), f32), in_spec...  198 us

profile of v3, /device:TPU:101, one launch (start us, length us, event | category | flops | bytes accessed | tf_op | source)
XLA Modules:
  0.0 200.8 jit_solution(13321860262901108134)
XLA Ops:
  0.0 197.7 %two_panels.1 = f32[1024,512]{1,0:T(8,128)} custom-call(f32[1024,512]{1,0:T(8,128)} %a_ref.1), custom_call_target="tpu_custom_call" | custom-call | flops 20000000000 | bytes 8000000 | tf_op jit(solution)/shard_map/two_panels/pallas_call | solution.py:832
  197.8 3.1 %copy.3 = f32[1024,512]{1,0:T(8,128)} copy(f32[1024,512]{1,0:T(8,128)} %two_panels.1) | data formatting | bytes 4194304

commit v4 on v3

--- a/solution.py
+++ b/solution.py
@@ -635,8 +635,9 @@
             d_second(1)
             work[0:B, 0:B] = D[0:B, 0:B]
 
-            def keep(rs, cs, value):
-                lref[rs, cs] = value
+            def keep(rs, cs, value, tile=True):
+                if tile:
+                    lref[rs, cs] = value
                 LW[rs, cs] = value
                 pair_ = split(value)
                 lh[rs, cs], ll[rs, cs] = pair_
@@ -671,10 +672,10 @@
                 def _():
                     w = close_root(1)
                     d_gather(1)
-                    es = keep(slice(T, W), q0, dot3(split(D[T:W, q0]), (wh[0], wl[0])))
+                    es = keep(slice(T, W), q0, dot3(split(D[T:W, q0]), (wh[0], wl[0])), False)
                     send(0)
                     rest = D[T:W, q1] - dot3(es, (lh[q1, q0], ll[q1, q0]))
-                    keep(slice(T, W), q1, dot3(split(rest), w))
+                    keep(slice(T, W), q1, dot3(split(rest), w), False)
                     send(1)
                     left = lambda r: (lh[r, 0:T], ll[r, 0:T])
                     work[q2, q2] = D[q2, q2] - dot3(left(q2), left(q2))
@@ -701,9 +702,12 @@
 
                 upper, inverse = chol_block(work[here, here])
                 wref[here, :] = inverse
-                ri = lax.broadcasted_iota(jnp.int32, (B, B), 0)
-                ci = lax.broadcasted_iota(jnp.int32, (B, B), 1)
-                lref[here, here] = jnp.where(ri >= ci, upper.T, 0.0)
+
+                @pl.when((row == first) & in_panel)
+                def _():
+                    ri = lax.broadcasted_iota(jnp.int32, (B, B), 0)
+                    ci = lax.broadcasted_iota(jnp.int32, (B, B), 1)
+                    lref[here, here] = jnp.where(ri >= ci, upper.T, 0.0)
 
             close_root(3)
             l_core(3).start()

time: 201 us -> 201 us (level)
  no operation moved by 1% of the time
where the time goes in v4:
time: 201 us
  Pallas kernels  198 us (99%)
  local copies, waits for them, and re-layouts  3.08 us (2%)
    pallas_call x1, Pallas kernels, local(): pl.pallas_call(body, out_shape=jax.ShapeDtypeStruct((W, T), f32), in_spec...  198 us

profile of v4, /device:TPU:101, one launch (start us, length us, event | category | flops | bytes accessed | tf_op | source)
XLA Modules:
  0.0 200.8 jit_solution(15845451757379500375)
XLA Ops:
  0.0 197.7 %two_panels.1 = f32[1024,512]{1,0:T(8,128)} custom-call(f32[1024,512]{1,0:T(8,128)} %a_ref.1), custom_call_target="tpu_custom_call" | custom-call | flops 20000000000 | bytes 8000000 | tf_op jit(solution)/shard_map/two_panels/pallas_call | solution.py:836
  197.7 3.1 %copy.3 = f32[1024,512]{1,0:T(8,128)} copy(f32[1024,512]{1,0:T(8,128)} %two_panels.1) | data formatting | bytes 4194304
